TPU v7x, 128 devices: a whole 4x4x4 slice. The times are simulated.
128 devices in a mesh: lat: 16 (over x, y), lev: 8 (over z, core).
Axes of the slice: x: 4, y: 4, z: 4, core: 2. Of those that a mesh axis runs over, the one named last changes fastest.
Arguments:
- fields: bfloat16 [64, 72, 16384], P('lat', None, 'lev'), may hold values from -6 to 6
- lat_order: int32 [64], replicated, may hold values from 0 to 63, each once
- counts: int32 [64], replicated, may hold values from 20 to 16016, as said below
- wave_order: int32 [2048], replicated, may hold values from 0 to 2047, as said below
- weights: float32 [64], replicated, may hold values from 0.3 to 3
- diffusion: float32 [3], replicated, may hold values from 0.5 to 8
- legendre: float32 [2048, 64, 2048], P(('lat', 'lev')), as said below
Outputs:
- fields_out: bfloat16 [64, 72, 16384], P('lat', None, 'lev')
Inputs may be any that keep to these rules, and one draw needn't show every extreme that they name: counts are 4 i + 20 for distinct hemisphere rows i below 4000, rising with the latitude index, the first one the row i = 0, the last one the row i = 3999. `wave_order`: a permutation; the device at position s of lat+lev (lat slowest) owns the wavenumbers at positions s * 2048 / 128 up to the next set's first. `legendre`: entry [r, j, q] is 0 where q >= 2048 - wave_order_r.
All inputs are finite; a program needn't handle non-finite values.
Results may differ from a plain program's by a relative error of at most 0.006.
Values may be sent and summed in bfloat16 or wider, within the bound.
A program may use at most 128 MiB of HBM per device.

v0:
```python
import math

import jax
import jax.numpy as jnp
from jax import lax
from jax.sharding import PartitionSpec as P

LEV = 24


full_turn = 2.0 * math.pi


def phase_table(wave_ids, row_count, positions, stride):
    turns = wave_ids[None, :] * (stride * positions[:, None]) % row_count
    return full_turn * turns.astype(jnp.float32) / row_count.astype(jnp.float32)


def basis_table(wave_ids, row_count):
    angle = phase_table(wave_ids, row_count, jnp.arange(128, dtype=jnp.int32), 1)
    return jnp.concatenate([jnp.cos(angle), -jnp.sin(angle)], axis=1).astype(jnp.bfloat16)


def forward_row(points, row_count, wave_ids):
    row_width = points.shape[-1]
    blocks = row_width // 128
    wave_count = wave_ids.shape[0]
    inside = jnp.arange(row_width, dtype=jnp.int32) < row_count
    masked = jnp.where(inside[None, :], points, jnp.zeros((), points.dtype))
    partial_value = jnp.dot(
        masked.reshape(-1, 128),
        basis_table(wave_ids, row_count),
        preferred_element_type=jnp.float32,
    )
    partial_value = partial_value.reshape(points.shape[0], blocks, 2 * wave_count)
    outer = phase_table(wave_ids, row_count, jnp.arange(blocks, dtype=jnp.int32), 128)
    cos_part, sin_part = (jnp.cos(outer), jnp.sin(outer))
    real_in, imag_in = (partial_value[..., :wave_count], partial_value[..., wave_count:])
    real_part = jnp.sum(real_in * cos_part + imag_in * sin_part, axis=1)
    imag_part = jnp.sum(imag_in * cos_part - real_in * sin_part, axis=1)
    cutoff = jnp.minimum(wave_count - 1, (row_count - 1) // 2)
    kept_share = jnp.where(wave_ids <= cutoff, 1.0, 0.0).astype(jnp.float32) / row_count.astype(
        jnp.float32
    )
    return jnp.stack([real_part, imag_part], axis=1) * kept_share


def inverse_row(coeffs, row_count, wave_ids, row_width):
    blocks = row_width // 128
    wave_count = wave_ids.shape[0]
    double = jnp.where(wave_ids == 0, 1.0, 2.0).astype(jnp.float32)
    real_in = coeffs[:, 0] * double
    imag_in = coeffs[:, 1] * double
    outer = phase_table(wave_ids, row_count, jnp.arange(blocks, dtype=jnp.int32), 128)
    cos_part, sin_part = (jnp.cos(outer), jnp.sin(outer))
    real_twist = real_in[:, None, :] * cos_part - imag_in[:, None, :] * sin_part
    imag_twist = real_in[:, None, :] * sin_part + imag_in[:, None, :] * cos_part
    twisted = jnp.concatenate([real_twist, imag_twist], axis=-1).astype(jnp.bfloat16)
    values = lax.dot_general(
        twisted.reshape(-1, 2 * wave_count),
        basis_table(wave_ids, row_count),
        (((1,), (1,)), ((), ())),
        preferred_element_type=jnp.float32,
    )
    values = values.reshape(coeffs.shape[0], row_width)
    inside = jnp.arange(row_width, dtype=jnp.int32) < row_count
    return jnp.where(inside[None, :], values, 0.0).astype(jnp.bfloat16)


def spectral_block(inputs, basis, wave_ids, counts, weights, diffusion, levels):
    batch_size, field_cols = (inputs.shape[0], inputs.shape[1])
    total = basis.shape[2]
    weighted = (inputs * weights).reshape(batch_size, 2 * field_cols, -1)
    spectral = jnp.einsum("icj,ijq->icq", weighted, basis, precision=lax.Precision.HIGHEST)
    degree = wave_ids[:, None] + jnp.arange(total, dtype=jnp.int32)[None, :]
    scaled_degree = (
        degree.astype(jnp.float32) * (degree + 1).astype(jnp.float32) / float(total * (total - 1))
    )
    column_field = jnp.arange(2 * field_cols, dtype=jnp.int32) // 2 // levels
    coefficient = jnp.take(diffusion, column_field)
    damping = 1.0 / (1.0 + coefficient[None, :, None] * (scaled_degree * scaled_degree)[:, None, :])
    returned = jnp.einsum(
        "icq,ijq->icj", spectral * damping, basis, precision=lax.Precision.HIGHEST
    )
    cutoff = jnp.minimum(total - 1, (counts - 1) // 2)
    kept_share = jnp.where(wave_ids[:, None] <= cutoff[None, :], 1.0, 0.0).astype(jnp.float32)
    return (returned * kept_share[:, None, :]).reshape(batch_size, field_cols, 2, -1)


def body(fields, lat_order, counts, wave_order, weights, diffusion, legendre):
    lat_sets = lax.axis_size("lat")
    lev_sets = lax.axis_size("lev")
    set_count = lat_sets * lev_sets
    rows_here = fields.shape[0]
    wave_count = wave_order.shape[0]
    each_set = wave_count // set_count
    lat_index = lax.axis_index("lat")
    own_latitudes = lax.dynamic_slice_in_dim(lat_order, lat_index * rows_here, rows_here)
    own_counts = jnp.take(counts, own_latitudes)
    full_rows = lax.all_to_all(fields, "lev", split_axis=1, concat_axis=2, tiled=True)
    level_cols = full_rows.shape[1]
    row_width = full_rows.shape[2]
    fourier = lax.map(
        lambda record: forward_row(record[0], record[1], wave_order), (full_rows, own_counts)
    )
    outgoing = (
        fourier.reshape(rows_here, level_cols, 2, set_count, each_set)
        .transpose(3, 4, 1, 2, 0)
        .reshape(set_count, -1)
    )
    incoming = lax.all_to_all(outgoing, ("lat", "lev"), split_axis=0, concat_axis=0, tiled=True)
    by_source = incoming.reshape(lat_sets, lev_sets, each_set, level_cols, 2, rows_here)
    by_slot = by_source.transpose(2, 1, 3, 4, 0, 5).reshape(
        each_set, lev_sets * level_cols, 2, lat_sets * rows_here
    )
    inverse = jnp.argsort(lat_order)
    by_latitude = jnp.take(by_slot, inverse, axis=3)
    own_set = lat_index * lev_sets + lax.axis_index("lev")
    own_waves = lax.dynamic_slice_in_dim(wave_order, own_set * each_set, each_set)
    returned = spectral_block(by_latitude, legendre, own_waves, counts, weights, diffusion, LEV)
    back_slot = jnp.take(returned, lat_order, axis=3)
    sending = (
        back_slot.reshape(each_set, lev_sets, level_cols, 2, lat_sets, rows_here)
        .transpose(4, 1, 0, 2, 3, 5)
        .reshape(set_count, -1)
    )
    arriving = lax.all_to_all(sending, ("lat", "lev"), split_axis=0, concat_axis=0, tiled=True)
    row_coeffs = (
        arriving.reshape(set_count, each_set, level_cols, 2, rows_here)
        .transpose(4, 2, 3, 0, 1)
        .reshape(rows_here, level_cols, 2, wave_count)
    )
    grid_rows = lax.map(
        lambda record: inverse_row(record[0], record[1], wave_order, row_width),
        (row_coeffs, own_counts),
    )
    return lax.all_to_all(grid_rows, "lev", split_axis=2, concat_axis=1, tiled=True)


def solution(mesh):
    placed = (P("lat", None, "lev"), P(), P(), P(), P(), P(), P(("lat", "lev"), None, None))
    return jax.shard_map(
        body, mesh=mesh, in_specs=placed, out_specs=P("lat", None, "lev"), check_vma=False
    )
```

profile of v0, /device:TPU:1, one launch (start us, length us, event | category | flops | bytes accessed | tf_op | source)
XLA Modules:
  0.0 672.3 jit_solution(1049102992856485995)
XLA Ops:
  0.0 3.2 copy.40
  3.2 6.8 %all-to-all-start = ((bf16[4,72,2048]{2,0,1:T(4,128)(2,1)}), bf16[4,72,2048]{2,0,1:T(4,128)(2,1)S(1)}, u32[]{:S(2)}, u32[]{:S(2)}) async-start(bf16[4,72,2048]{2,0,1:T(4,128)(2,1)} %copy.40), calls=%async_computation | async-start | bytes 2359296 | tf_op jit(solution)/shard_map/all_to_all | solution.py:100
  21.7 4.8 all-to-all-done
  27.9 184.4 %while.23 = (s32[]{:T(128)}, f32[4,9,2,2048]{3,2,1,0:T(2,128)}, s32[4]{0:T(128)S(1)}, bf16[4,9,16384]{2,1,0:T(8,128)(2,1)S(1)}, s32[2048]{0:T(1024)S(1)}, /*index=5*/s32[]{:T(128)}, s32[]{:T(128)}, s32[]{:T(128)}, s32[]{:T(128)}) while((s32[]{:T(128)}, f32[4,9,2,2048]{3,2,1,0:T(2,128)}, s32[4]{0:T(128)S(1)}, ...), condition=%wide.region_3.4_spmd, body=%wide.region_0.3_spmd.sunk | while | flops 1235724416 | bytes 46778192 | solution.py:103
  53.1 27.8 %fusion.74 = (f32[128,2048]{1,0:T(8,128)S(1)}, f32[128,2048]{1,0:T(8,128)S(1)}, bf16[128,2048]{1,0:T(8,128)(2,1)S(1)}, bf16[128,2048]{1,0:T(8,128)(2,1)S(1)}) fusion(f32[]{:T(128)S(6)} %convert_element_type.130, pred[]{:T(512)S(6)} %lt.217, s32[]{:T(128)S(6)} %select_n.320, s32[128]{0:T(128)S(1)} %iota_multiply_fusion.4, s32[2048]{0:T(1024)S(1)} %get-tuple-element.293), kind=kLoop, calls=%fused_computation.30.clone.1 | loop fusion | flops 6553600 | bytes 3154441 | tf_op jit(solution)/shard_map/while/body/eval_jaxpr/cos | solution.py:37
  91.5 27.8 %fusion.74 = (f32[128,2048]{1,0:T(8,128)S(1)}, f32[128,2048]{1,0:T(8,128)S(1)}, bf16[128,2048]{1,0:T(8,128)(2,1)S(1)}, bf16[128,2048]{1,0:T(8,128)(2,1)S(1)}) fusion(f32[]{:T(128)S(6)} %convert_element_type.130, pred[]{:T(512)S(6)} %lt.217, s32[]{:T(128)S(6)} %select_n.320, s32[128]{0:T(128)S(1)} %iota_multiply_fusion.4, s32[2048]{0:T(1024)S(1)} %get-tuple-element.293), kind=kLoop, calls=%fused_computation.30.clone.1 | loop fusion | flops 6553600 | bytes 3154441 | tf_op jit(solution)/shard_map/while/body/eval_jaxpr/cos | solution.py:37
  129.9 27.8 %fusion.74 = (f32[128,2048]{1,0:T(8,128)S(1)}, f32[128,2048]{1,0:T(8,128)S(1)}, bf16[128,2048]{1,0:T(8,128)(2,1)S(1)}, bf16[128,2048]{1,0:T(8,128)(2,1)S(1)}) fusion(f32[]{:T(128)S(6)} %convert_element_type.130, pred[]{:T(512)S(6)} %lt.217, s32[]{:T(128)S(6)} %select_n.320, s32[128]{0:T(128)S(1)} %iota_multiply_fusion.4, s32[2048]{0:T(1024)S(1)} %get-tuple-element.293), kind=kLoop, calls=%fused_computation.30.clone.1 | loop fusion | flops 6553600 | bytes 3154441 | tf_op jit(solution)/shard_map/while/body/eval_jaxpr/cos | solution.py:37
  168.3 27.8 %fusion.74 = (f32[128,2048]{1,0:T(8,128)S(1)}, f32[128,2048]{1,0:T(8,128)S(1)}, bf16[128,2048]{1,0:T(8,128)(2,1)S(1)}, bf16[128,2048]{1,0:T(8,128)(2,1)S(1)}) fusion(f32[]{:T(128)S(6)} %convert_element_type.130, pred[]{:T(512)S(6)} %lt.217, s32[]{:T(128)S(6)} %select_n.320, s32[128]{0:T(128)S(1)} %iota_multiply_fusion.4, s32[2048]{0:T(1024)S(1)} %get-tuple-element.293), kind=kLoop, calls=%fused_computation.30.clone.1 | loop fusion | flops 6553600 | bytes 3154441 | tf_op jit(solution)/shard_map/while/body/eval_jaxpr/cos | solution.py:37
  212.3 4.3 reshape.471
  220.9 8.0 %all-to-all-start.1 = ((f32[128,1,1152]{2,1,0:T(1,128)}), f32[128,1,1152]{2,1,0:T(1,128)S(1)}, u32[]{:S(2)}, u32[]{:S(2)}) async-start(f32[128,1,1152]{2,1,0:T(1,128)} %copy.44), calls=%async_computation.1 | async-start | bytes 1179648 | tf_op jit(solution)/shard_map/all_to_all | solution.py:111
  229.0 14.2 %all-to-all-done.1 = f32[128,1,1152]{2,1,0:T(1,128)S(1)} async-done(((f32[128,1,1152]{2,1,0:T(1,128)}), f32[128,1,1152]{2,1,0:T(1,128)S(1)}, u32[]{:S(2)}, u32[]{:S(2)}) %all-to-all-start.1) | async-done | bytes 589856 | tf_op jit(solution)/shard_map/all_to_all | solution.py:111
  243.9 6.7 reshape.472
  250.6 9.7 %copy.46 = f32[16,8,9,2,16,4]{0,5,4,3,2,1:T(4,128)} copy(f32[16,8,9,2,16,4]{1,4,5,3,2,0:T(8,128)} %bitcast.81) | data formatting | bytes 1179648 | tf_op jit(solution)/shard_map/transpose | solution.py:113
  260.4 5.5 copy.47
  267.9 19.3 %fusion.60 = f32[16,144,2048]{2,1,0:T(8,128)} fusion(f32[16,64,2048]{2,1,0:T(8,128)} %param.19, f32[16,144,64]{2,0,1:T(8,128)S(1)} %bitcast.85), kind=kOutput, calls=%fused_computation.93 | convolution fusion | flops 3623878656 | bytes 27852800 | tf_op jit(solution)/shard_map/icj,ijq->icq/dot_general | solution.py:74
  287.2 27.7 %fusion.57 = f32[16,144,64]{1,2,0:T(8,128)S(1)} fusion(f32[16,64,2048]{2,1,0:T(8,128)} %param.19, f32[16,144,2048]{2,1,0:T(8,128)} %fusion.60, f32[16,2048]{1,0:T(8,128)S(1)} %multiply_multiply_fusion, f32[144]{0:T(256)S(1)} %and_select_fusion.3, f32[16,64]{1,0:T(8,128)S(1)} %compare_select_fusion.1), kind=kOutput, calls=%fused_computation.92 | convolution fusion | flops 3642900480 | bytes 27988544 | tf_op jit(solution)/shard_map/icq,ijq->icj/dot_general | solution.py:82
  317.4 4.9 copy.52
  322.2 10.8 %copy.53 = f32[16,8,16,9,2,4]{1,0,5,4,3,2:T(8,128)} copy(f32[16,8,16,9,2,4]{2,5,0,4,3,1:T(4,128)} %bitcast.83) | data formatting | bytes 1179648 | tf_op jit(solution)/shard_map/transpose | solution.py:124
  333.1 7.0 %all_to_all.44 = f32[128,1,1152]{0,2,1:T(8,128)S(1)} reshape(f32[16,8,16,9,2,4]{1,0,5,4,3,2:T(8,128)} %copy.53) | data formatting | bytes 1179648 | tf_op jit(solution)/shard_map/all_to_all | solution.py:127
  341.3 4.6 all-to-all-start.2
  345.9 14.5 %all-to-all-done.2 = f32[128,1,1152]{2,1,0:T(1,128)S(1)} async-done(((f32[128,1,1152]{2,1,0:T(1,128)}), f32[128,1,1152]{2,1,0:T(1,128)S(1)}, u32[]{:S(2)}, u32[]{:S(2)}) %all-to-all-start.2) | async-done | bytes 589856 | tf_op jit(solution)/shard_map/all_to_all | solution.py:127
  364.0 4.3 reshape.478
  368.4 179.0 %while.24 = (s32[]{:T(128)}, bf16[4,9,16384]{2,1,0:T(8,128)(2,1)}, s32[4]{0:T(128)S(1)}, f32[4,9,2,2048]{3,2,1,0:T(2,128)S(1)}, s32[2048]{0:T(1024)S(1)}, /*index=5*/s32[]{:T(128)}, s32[]{:T(128)}) while((s32[]{:T(128)}, bf16[4,9,16384]{2,1,0:T(8,128)(2,1)}, s32[4]{0:T(128)S(1)}, f32[4,9,2,2048]{3,2,1,0:T(2,128)S(1)}, s32[2048]{0:T(1024)S(1)}, ...), condition=%wide.region_6.8_spmd, body=%wide.region_5.7_spmd.sunk | while | flops 1254563968 | bytes 27969168 | solution.py:133
  393.3 27.8 %cosine_convert_fusion.3 = (bf16[128,2048]{1,0:T(8,128)(2,1)S(1)}, bf16[128,2048]{1,0:T(8,128)(2,1)S(1)}, f32[128,2048]{1,0:T(8,128)S(1)}, f32[128,2048]{1,0:T(8,128)S(1)}) fusion(f32[]{:T(128)S(6)} %convert_element_type.132, pred[]{:T(512)S(6)} %lt.221, s32[]{:T(128)S(6)} %select_n.325, s32[2048]{0:T(1024)S(1)} %get-tuple-element.316, ...), kind=kLoop, calls=%fused_computation.61.clone.1 | loop fusion | flops 6553600 | bytes 3154441 | tf_op jit(solution)/shard_map/convert
  430.9 27.8 %cosine_convert_fusion.3 = (bf16[128,2048]{1,0:T(8,128)(2,1)S(1)}, bf16[128,2048]{1,0:T(8,128)(2,1)S(1)}, f32[128,2048]{1,0:T(8,128)S(1)}, f32[128,2048]{1,0:T(8,128)S(1)}) fusion(f32[]{:T(128)S(6)} %convert_element_type.132, pred[]{:T(512)S(6)} %lt.221, s32[]{:T(128)S(6)} %select_n.325, s32[2048]{0:T(1024)S(1)} %get-tuple-element.316, ...), kind=kLoop, calls=%fused_computation.61.clone.1 | loop fusion | flops 6553600 | bytes 3154441 | tf_op jit(solution)/shard_map/convert
  468.5 27.8 %cosine_convert_fusion.3 = (bf16[128,2048]{1,0:T(8,128)(2,1)S(1)}, bf16[128,2048]{1,0:T(8,128)(2,1)S(1)}, f32[128,2048]{1,0:T(8,128)S(1)}, f32[128,2048]{1,0:T(8,128)S(1)}) fusion(f32[]{:T(128)S(6)} %convert_element_type.132, pred[]{:T(512)S(6)} %lt.221, s32[]{:T(128)S(6)} %select_n.325, s32[2048]{0:T(1024)S(1)} %get-tuple-element.316, ...), kind=kLoop, calls=%fused_computation.61.clone.1 | loop fusion | flops 6553600 | bytes 3154441 | tf_op jit(solution)/shard_map/convert
  506.2 27.8 %cosine_convert_fusion.3 = (bf16[128,2048]{1,0:T(8,128)(2,1)S(1)}, bf16[128,2048]{1,0:T(8,128)(2,1)S(1)}, f32[128,2048]{1,0:T(8,128)S(1)}, f32[128,2048]{1,0:T(8,128)S(1)}) fusion(f32[]{:T(128)S(6)} %convert_element_type.132, pred[]{:T(512)S(6)} %lt.221, s32[]{:T(128)S(6)} %select_n.325, s32[2048]{0:T(1024)S(1)} %get-tuple-element.316, ...), kind=kLoop, calls=%fused_computation.61.clone.1 | loop fusion | flops 6553600 | bytes 3154441 | tf_op jit(solution)/shard_map/convert
  547.4 19.9 %copy.57 = bf16[4,9,16384]{1,0,2:T(4,128)(2,1)} copy(bf16[4,9,16384]{2,1,0:T(8,128)(2,1)} %get-tuple-element.120) | data formatting | bytes 2359296 | tf_op jit(solution)/shard_map/while | solution.py:133
  567.3 25.9 %reshape.533 = bf16[8,2,36864]{2,1,0:T(2,128)(2,1)S(1)} reshape(bf16[16384,4,9]{2,1,0:T(4,128)(2,1)} %bitcast.77) | data formatting | bytes 2359296
  593.3 20.2 %all_to_all.54 = bf16[8,2,36864]{2,1,0:T(2,128)(2,1)S(1)} all-to-all(bf16[8,2,36864]{2,1,0:T(2,128)(2,1)S(1)} %reshape.533), channel_id=1, replica_groups=mesh['lat'=16,'lev'=8] {'lev'}, dimensions={0} | all-to-all | bytes 2359296 | tf_op jit(solution)/shard_map/all_to_all | solution.py:137
  613.5 39.3 %reshape.534 = bf16[16384,4,9]{2,1,0:T(4,128)(2,1)} reshape(bf16[8,2,36864]{2,1,0:T(2,128)(2,1)S(1)} %all_to_all.54) | data formatting | bytes 2359296
  652.8 16.7 %copy.62 = bf16[4,9,8,2048]{3,2,0,1:T(8,128)(2,1)S(1)} copy(bf16[4,9,8,2048]{1,0,3,2:T(4,128)(2,1)} %bitcast.78) | data formatting | bytes 2359296 | tf_op jit(solution)/shard_map/all_to_all | solution.py:137
  (130 shorter events, 92.6 us)
Async XLA Ops:
  0.0 27.9 %copy-start = (s32[2048]{0:T(1024)S(1)}, s32[2048]{0:T(1024)}, u32[]{:S(2)}) copy-start(s32[2048]{0:T(1024)} %param.16) | copy-start | bytes 24580
  3.2 23.3 %all-to-all-start = ((bf16[4,72,2048]{2,0,1:T(4,128)(2,1)}), bf16[4,72,2048]{2,0,1:T(4,128)(2,1)S(1)}, u32[]{:S(2)}, u32[]{:S(2)}) async-start(bf16[4,72,2048]{2,0,1:T(4,128)(2,1)} %copy.40), calls=%async_computation | async-start | bytes 2359296 | tf_op jit(solution)/shard_map/all_to_all | solution.py:100
  220.9 22.4 %all-to-all-start.1 = ((f32[128,1,1152]{2,1,0:T(1,128)}), f32[128,1,1152]{2,1,0:T(1,128)S(1)}, u32[]{:S(2)}, u32[]{:S(2)}) async-start(f32[128,1,1152]{2,1,0:T(1,128)} %copy.44), calls=%async_computation.1 | async-start | bytes 1179648 | tf_op jit(solution)/shard_map/all_to_all | solution.py:111
  250.6 15.9 %copy-start.1 = (f32[64]{0:T(128)S(1)}, f32[64]{0:T(128)}, u32[]{:S(2)}) copy-start(f32[64]{0:T(128)} %param.17) | copy-start | bytes 772
  341.3 19.1 %all-to-all-start.2 = ((f32[128,1,1152]{2,1,0:T(1,128)}), f32[128,1,1152]{2,1,0:T(1,128)S(1)}, u32[]{:S(2)}, u32[]{:S(2)}) async-start(f32[128,1,1152]{2,1,0:T(1,128)} %copy.54), calls=%async_computation.2 | async-start | bytes 1179648 | tf_op jit(solution)/shard_map/all_to_all | solution.py:127
where the time goes:
time: 677 us; the launch traced here: 672 us
  other arithmetic  266 us (39%)
  local copies, waits for them, and re-layouts  186 us (27%)
  loops' own time  78.2 us (12%)
  matrix products  67.9 us (10%)
  waiting for transfers between devices  33.5 us (5%)
  blocking collectives  20.2 us (3%)
  starting transfers between devices  19.4 us (3%)
    another operation x8, other arithmetic  122 us
    cos x4, other arithmetic, forward_row(): cos_part, sin_part = (jnp.cos(outer), jnp.sin(outer))  111 us
    unnamed x7, local copies, waits for them, and re-layouts  68.5 us
    another operation x1, loops' own time, body(): lax.map(lambda record: forward_row(record[0], record[1], wave_order), (fu...  41.6 us
    another operation x1, loops' own time, body(): lax.map(lambda record: inverse_row(record[0], record[1], wave_order, row_...  36.6 us
    dot_general x1, matrix products, spectral_block(): jnp.einsum('icq,ijq->icj', spectral * damping, basis, precision=lax.Preci...  27.7 us
    all_to_all x1, blocking collectives, body(): lax.all_to_all(grid_rows, 'lev', split_axis=2, concat_axis=1, tiled=True)  20.2 us
    while x1, local copies, waits for them, and re-layouts, body(): lax.map(lambda record: inverse_row(record[0], record[1], wave_order, row_...  19.9 us
  transfers between devices with their start and end apart: 3, of which 3 were waited for; matrix products, arithmetic and copies ran while one was open for 2% of the time, Pallas kernels for 0%

commit v1 on v0

v1 whole, which is shorter than its diff:
```python
import math

import jax
import jax.numpy as jnp
from jax import lax
from jax.experimental import pallas as pl
from jax.experimental.pallas import tpu as pltpu
from jax.sharding import PartitionSpec as P

F32, BF16 = jnp.float32, jnp.bfloat16
MESH = pl.DeviceIdType.MESH

M = 2048
N_LAT, N_LEV = 16, 8
DEV = N_LAT * N_LEV
NLAT = 64
LEV = 24
FL = 72
HALF = FL // 2
ROWS = NLAT // N_LAT
PTS = 2048
K0 = 256
KK = PTS // K0
PAIRS = KK // 2
BLK = KK * HALF
EACH = M // DEV
WT = 256
LANES = 128


def nt_dot(a, b):
    return lax.dot_general(a, b, (((1,), (1,)), ((), ())), preferred_element_type=F32)


def sincos(wave, factor, count):
    product = wave * factor
    countf = count.astype(F32)
    turns = jnp.floor(product.astype(F32) * (1.0 / countf) + 0.5).astype(jnp.int32)
    rest = product - turns * count
    rest = jnp.where(2 * rest > count, rest - count, rest)
    rest = jnp.where(2 * rest < -count, rest + count, rest)
    z = rest.astype(F32) * (math.pi / countf)
    y = z * z
    s = jnp.full_like(y, 1.0 / math.factorial(13))
    for k in (11, 9, 7, 5, 3, 1):
        s = s * y + (-1.0) ** (k // 2) / math.factorial(k)
    s = s * z
    c = jnp.full_like(y, 1.0 / math.factorial(14) * -1.0)
    for k in (12, 10, 8, 6, 4, 2, 0):
        c = c * y + (-1.0) ** (k // 2) / math.factorial(k)
    return 1.0 - 2.0 * s * s, 2.0 * s * c


def kernel(
    lat_s, cnt_s, wave_s, wgt_s, dif_s, wave_v, fields, leg_hbm, out,
    leg, tmp, stage, xs, xr, basis, twc, tws, ebc, ebs, eac, eas, one,
    accr, acci, ft, fs, fr, x32, y32, rs, rr, pm, cn, wt, bs, gst, ur, ui, ys, yr, o32,
    leg_sem, xs_sem, xr_sem, fs_sem, fr_sem, rs_sem, rr_sem, ys_sem, yr_sem,
):
    lat, lev = lax.axis_index("lat"), lax.axis_index("lev")
    me = lat * N_LEV + lev
    z, core = lev // 2, lax.rem(lev, 2)

    barrier = pltpu.get_barrier_semaphore()

    def greet(d, carry):
        target = lax.rem(me + d, DEV)
        pl.semaphore_signal(
            barrier, inc=1, device_id=(target // N_LEV, lax.rem(target, N_LEV)), device_id_type=MESH
        )
        return carry

    lax.fori_loop(1, DEV, greet, 0)
    leg_copy = pltpu.make_async_copy(leg_hbm, leg, leg_sem)
    leg_copy.start()

    lane = lax.broadcasted_iota(jnp.int32, (FL, K0), 1)

    def stage_row(t, carry):
        count = cnt_s[lat_s[ROWS * lat + t]]
        for kk in range(KK):
            x = fields[t, :, kk * K0 : (kk + 1) * K0].astype(F32)
            tmp[kk % 2] = jnp.where(lane + (lev * PTS + kk * K0) < count, x, 0.0)
            for h in range(2):
                stage[h, kk * HALF : (kk + 1) * HALF, :] = tmp[kk % 2, h * HALF : (h + 1) * HALF, :]
        for h in range(2):
            xs[2 * t + h] = stage[h].astype(BF16)
        return carry

    lax.fori_loop(0, ROWS, stage_row, 0)

    pl.semaphore_wait(barrier, DEV - 1)

    def x_copy(target, slot_sem_src, source):
        return pltpu.make_async_remote_copy(
            src_ref=xs.at[target],
            dst_ref=xr.at[source],
            send_sem=xs_sem.at[target],
            recv_sem=xr_sem.at[source],
            device_id=(lat, target),
            device_id_type=MESH,
        )

    def send_x(d, carry):
        target = lax.rem(lev + d, N_LEV)
        x_copy(target, None, lev).start()
        return carry

    lax.fori_loop(1, N_LEV, send_x, 0)

    count = cnt_s[lat_s[ROWS * lat + z]]
    waves16 = jnp.broadcast_to(wave_v[...], (16, M))
    row16 = lax.broadcasted_iota(jnp.int32, (16, M), 0)
    ebc[...], ebs[...] = sincos(waves16, row16, count)
    eac[...], eas[...] = sincos(waves16, row16 * 16, count)
    twc[0:16], tws[0:16] = sincos(waves16, row16 * (2 * K0), count)
    twc[16:32], tws[16:32] = sincos(waves16, row16 * (2 * K0) + 32 * K0, count)
    waves8 = jnp.broadcast_to(wave_v[...], (8, M))
    one[0], one[1] = sincos(waves8, jnp.full((8, M), K0, jnp.int32), count)

    def basis_rows(a, carry):
        ca, sa = eac[pl.ds(a, 1), :], eas[pl.ds(a, 1), :]
        cb, sb = ebc[...], ebs[...]
        rows = pl.ds(pl.multiple_of(a * 16, 16), 16)
        basis[rows, 0:M] = (ca * cb - sa * sb).astype(BF16)
        basis[rows, M : 2 * M] = (-(sa * cb + ca * sb)).astype(BF16)
        return carry

    lax.fori_loop(0, 16, basis_rows, 0)

    lane64 = lax.broadcasted_iota(jnp.int32, (1, NLAT), 1)

    def slot_row(t, carry):
        j = lat_s[t]
        row = pl.ds(t, 1)
        pm[row, :] = jnp.where(lane64 == j, 1.0, 0.0)
        cn[row, :] = jnp.full((1, NLAT), cnt_s[j], jnp.int32).astype(F32)
        wt[row, :] = jnp.full((1, NLAT), wgt_s[j], F32)
        return carry

    lax.fori_loop(0, NLAT, slot_row, 0)
    eye = lax.broadcasted_iota(jnp.int32, (NLAT, NLAT), 0) == lax.broadcasted_iota(
        jnp.int32, (NLAT, NLAT), 1
    )
    count_col = cn[...]
    count_row = jnp.sum(jnp.where(eye, count_col, 0.0), axis=0, keepdims=True)
    share_row = jnp.sum(jnp.where(eye, wt[...], 0.0), axis=0, keepdims=True) / count_row
    perm = pm[...].astype(BF16)
    degree = lax.broadcasted_iota(jnp.int32, (1, M), 1)
    leg_copy.wait()

    def operator(i, carry):
        m = wave_s[me * EACH + i]
        n = (degree + m).astype(F32)
        scaled = n * (n + 1.0) * (1.0 / float(M * (M - 1)))
        scaled = scaled * scaled
        own = jnp.dot(perm, leg[i].astype(BF16), preferred_element_type=F32)
        for f in range(3):
            bs[f * NLAT : (f + 1) * NLAT, :] = (own * (1.0 / (1.0 + dif_s[f] * scaled))).astype(BF16)
        g = nt_dot(bs[...], own.astype(BF16))
        twice_m = (2 * jnp.full((1, NLAT), m, jnp.int32)).astype(F32)
        from_row = jnp.where(twice_m < count_row, share_row, 0.0)
        to_col = jnp.where(twice_m < count_col, jnp.where(twice_m == 0.0, 1.0, 2.0), 0.0)
        scale = to_col * from_row
        for f in range(3):
            gst[i, f * NLAT : (f + 1) * NLAT, :] = (g[f * NLAT : (f + 1) * NLAT, :] * scale).astype(BF16)
        return carry

    lax.fori_loop(0, EACH, operator, 0)

    accr[...] = jnp.zeros_like(accr)
    acci[...] = jnp.zeros_like(acci)
    xr[lev] = xs[lev]

    def forward(p):
        points = xr[p]
        for w in range(M // WT):
            cols = slice(w * WT, (w + 1) * WT)
            pr = jnp.dot(points, basis[:, cols], preferred_element_type=F32)
            pi = jnp.dot(points, basis[:, M + w * WT : M + (w + 1) * WT], preferred_element_type=F32)
            ar, ai = accr[:, cols], acci[:, cols]
            for k in range(PAIRS):
                c = twc[pl.ds(p * PAIRS + k, 1), cols]
                s = tws[pl.ds(p * PAIRS + k, 1), cols]
                br, bi = pr[k * FL : (k + 1) * FL], pi[k * FL : (k + 1) * FL]
                ar = ar + (br * c + bi * s)
                ai = ai + (bi * c - br * s)
            accr[:, cols] = ar
            acci[:, cols] = ai

    forward(lev)

    def arrived(step, carry):
        chip_step = step // 2
        far = jnp.where(chip_step == 0, 0, jnp.where(chip_step == 1, 1, jnp.where(chip_step == 2, 3, 2)))
        p = 2 * lax.rem(z + far, 4) + lax.rem(core + lax.rem(step, 2), 2)
        x_copy(p, None, p).wait_recv()
        forward(p)
        return carry

    lax.fori_loop(1, N_LEV, arrived, 0)

    ft[FL:LANES, :] = jnp.zeros((LANES - FL, M), F32)
    c1, s1 = one[0, 0:1, :], one[1, 0:1, :]
    odd_r, odd_i = accr[HALF:FL, :], acci[HALF:FL, :]
    ft[0:HALF, :] = accr[0:HALF, :] + (odd_r * c1 + odd_i * s1)
    ft[HALF:FL, :] = acci[0:HALF, :] + (odd_i * c1 - odd_r * s1)
    for w in range(M // LANES):
        fs[w * LANES : (w + 1) * LANES, :] = ft[:, w * LANES : (w + 1) * LANES].T.astype(BF16)

    def tile(index):
        return pl.ds(pl.multiple_of(index * EACH, EACH), EACH)

    def send_tiles(source, target_ref, send_sem, recv_sem):
        def step(d, carry):
            target = lax.rem(me + d, DEV)
            pltpu.make_async_remote_copy(
                src_ref=source.at[tile(target), :],
                dst_ref=target_ref.at[tile(me), :],
                send_sem=send_sem,
                recv_sem=recv_sem,
                device_id=(target // N_LEV, lax.rem(target, N_LEV)),
                device_id_type=MESH,
            ).start()
            return carry

        lax.fori_loop(1, DEV, step, 0)
        target_ref[tile(me), :] = source[tile(me), :]

    def all_tiles(source, target_ref, send_sem, recv_sem):
        whole = pl.ds(0, (DEV - 1) * EACH)
        return pltpu.make_async_remote_copy(
            src_ref=source.at[whole, :],
            dst_ref=target_ref.at[whole, :],
            send_sem=send_sem,
            recv_sem=recv_sem,
            device_id=(lat, lax.rem(lev + 1, N_LEV)),
            device_id_type=MESH,
        )

    send_tiles(fs, fr, fs_sem, fr_sem)
    all_tiles(fs, fr, fs_sem, fr_sem).wait_recv()

    x32[...] = fr[...].astype(F32)
    column = lax.broadcasted_iota(jnp.int32, (NLAT, LANES), 1)
    column = jnp.where(column >= HALF, column - HALF, column)
    first_low, first_high = column < LEV, column < 2 * LEV - HALF
    for i in range(EACH):
        low = x32[pl.ds(i, NLAT, stride=2 * EACH), :]
        high = x32[pl.ds(EACH + i, NLAT, stride=2 * EACH), :]
        both = jnp.concatenate([low, high], axis=1).astype(BF16)
        y = jnp.dot(gst[i], both, preferred_element_type=F32)
        y32[pl.ds(i, NLAT, stride=2 * EACH), :] = jnp.where(
            first_low, y[0:NLAT, 0:LANES], y[NLAT : 2 * NLAT, 0:LANES]
        )
        y32[pl.ds(EACH + i, NLAT, stride=2 * EACH), :] = jnp.where(
            first_high, y[NLAT : 2 * NLAT, LANES:], y[2 * NLAT :, LANES:]
        )
    rs[...] = y32[...].astype(BF16)
    send_tiles(rs, rr, rs_sem, rr_sem)
    all_tiles(rs, rr, rs_sem, rr_sem).wait_recv()

    for w in range(M // LANES):
        cols = slice(w * LANES, (w + 1) * LANES)
        ft[:, cols] = rr[cols, :].astype(F32).T
    re, im = ft[0:HALF, :], ft[HALF:FL, :]
    ur[0:HALF, :] = re
    ui[0:HALF, :] = im
    ur[HALF:FL, :] = re * c1 - im * s1
    ui[HALF:FL, :] = re * s1 + im * c1

    row = lax.broadcasted_iota(jnp.int32, (BLK, K0), 0)
    point = lax.broadcasted_iota(jnp.int32, (BLK, K0), 1)
    for kk in range(1, KK):
        point = point + jnp.where(row >= kk * HALF, K0, 0)

    def inverse(p):
        total = jnp.zeros((BLK, K0), F32)
        for w in range(M // WT):
            cols = slice(w * WT, (w + 1) * WT)
            vr, vi = ur[:, cols], ui[:, cols]
            tr, ti = [], []
            for k in range(PAIRS):
                c = twc[pl.ds(p * PAIRS + k, 1), cols]
                s = tws[pl.ds(p * PAIRS + k, 1), cols]
                tr.append(vr * c - vi * s)
                ti.append(vr * s + vi * c)
            total = total + nt_dot(jnp.concatenate(tr, axis=0).astype(BF16), basis[:, cols])
            total = total + nt_dot(
                jnp.concatenate(ti, axis=0).astype(BF16), basis[:, M + w * WT : M + (w + 1) * WT]
            )
        ys[p] = jnp.where(point + p * PTS < count, total, 0.0).astype(BF16)

    def y_copy(target, source):
        return pltpu.make_async_remote_copy(
            src_ref=ys.at[target],
            dst_ref=yr.at[source],
            send_sem=ys_sem.at[target],
            recv_sem=yr_sem.at[source],
            device_id=(lat, target),
            device_id_type=MESH,
        )

    def made(step, carry):
        chip_step = step // 2
        far = jnp.where(chip_step == 0, 2, jnp.where(chip_step == 1, 1, jnp.where(chip_step == 2, 3, 0)))
        p = 2 * lax.rem(z + far, 4) + lax.rem(core + 1 + lax.rem(step, 2), 2)
        inverse(p)
        y_copy(p, lev).start()
        return carry

    lax.fori_loop(0, N_LEV - 1, made, 0)
    inverse(lev)
    yr[lev] = ys[lev]

    def waited(d, carry):
        y_copy(0, lax.rem(lev + d, N_LEV)).wait_recv()
        return carry

    lax.fori_loop(1, N_LEV, waited, 0)

    def finish_row(t, carry):
        for h in range(2):
            stage[h] = yr[2 * t + h].astype(F32)
        for kk in range(KK):
            for h in range(2):
                o32[h * HALF : (h + 1) * HALF, kk * K0 : (kk + 1) * K0] = stage[
                    h, kk * HALF : (kk + 1) * HALF, :
                ]
        out[t] = o32[...].astype(BF16)
        return carry

    lax.fori_loop(0, ROWS, finish_row, 0)

    def sent(d, carry):
        target = lax.rem(lev + d, N_LEV)
        x_copy(target, None, lev).wait_send()
        y_copy(target, lev).wait_send()
        return carry

    lax.fori_loop(1, N_LEV, sent, 0)
    all_tiles(fs, fr, fs_sem, fr_sem).wait_send()
    all_tiles(rs, rr, rs_sem, rr_sem).wait_send()


def body(fields, lat_order, counts, wave_order, weights, diffusion, legendre):
    smem, vmem = pl.BlockSpec(memory_space=pltpu.SMEM), pl.BlockSpec(memory_space=pltpu.VMEM)
    dma = pltpu.SemaphoreType.DMA
    block = pltpu.VMEM((N_LEV, BLK, K0), BF16)
    tiles16 = pltpu.VMEM((M, LANES), BF16)
    tiles32 = pltpu.VMEM((M, LANES), F32)
    acc = pltpu.VMEM((FL, M), F32)
    table = pltpu.VMEM((16, M), F32)
    square = pltpu.VMEM((NLAT, NLAT), F32)
    return pl.pallas_call(
        kernel,
        out_shape=jax.ShapeDtypeStruct(fields.shape, BF16),
        in_specs=[smem] * 5 + [vmem, vmem, pl.BlockSpec(memory_space=pl.ANY)],
        out_specs=vmem,
        scratch_shapes=[
            pltpu.VMEM((EACH, NLAT, M), F32),
            pltpu.VMEM((2, FL, K0), F32),
            pltpu.VMEM((2, BLK, K0), F32),
            block, block,
            pltpu.VMEM((K0, 2 * M), BF16),
            pltpu.VMEM((32, M), F32), pltpu.VMEM((32, M), F32),
            table, table, table, table,
            pltpu.VMEM((2, 8, M), F32),
            acc, acc,
            pltpu.VMEM((LANES, M), F32),
            tiles16, tiles16, tiles32, tiles32, tiles16, tiles16,
            square, square, square,
            pltpu.VMEM((3 * NLAT, M), BF16),
            pltpu.VMEM((EACH, 3 * NLAT, NLAT), BF16),
            acc, acc,
            block, block,
            acc,
            dma,
            dma((N_LEV,)), dma((N_LEV,)),
            dma, dma, dma, dma,
            dma((N_LEV,)), dma((N_LEV,)),
        ],
        compiler_params=pltpu.CompilerParams(
            collective_id=0, has_side_effects=True, vmem_limit_bytes=56 * 1024 * 1024
        ),
        cost_estimate=pl.CostEstimate(
            flops=20_000_000_000, bytes_accessed=12_000_000, transcendentals=0
        ),
    )(lat_order, counts, wave_order, weights, diffusion, wave_order.reshape(1, M), fields, legendre)


def solution(mesh):
    placed = (P("lat", None, "lev"), P(), P(), P(), P(), P(), P(("lat", "lev"), None, None))
    return jax.shard_map(
        body, mesh=mesh, in_specs=placed, out_specs=P("lat", None, "lev"), check_vma=False
    )
```

time: 677 us -> 75.8 us (0.11)
  other arithmetic: 266 us -> 0 us
  local copies, waits for them, and re-layouts: 186 us -> 2.41 us
  loops' own time: 78.2 us -> 0 us
  Pallas kernels: 0 us -> 73.2 us
  matrix products: 67.9 us -> 0 us
  waiting for transfers between devices: 33.5 us -> 0 us
  blocking collectives: 20.2 us -> 0 us
  starting transfers between devices: 19.4 us -> 0 us
    another operation x8 -> x0, other arithmetic: 122 us -> none
    cos x4 -> x0, other arithmetic: 111 us -> none  [forward_row(): cos_part, sin_part = (jnp.cos(outer), jnp.sin(outer))]
    another operation x2 -> x0, loops' own time: 78.2 us -> none  [the longest x1 41.6 us: body(): lax.map(lambda record: forward_row(record[0], record[1], wave_order), (fu...]
    pallas_call x0 -> x1, Pallas kernels: none -> 73.2 us  [body(): pl.pallas_call(kernel, out_shape=jax.ShapeDtypeStruct(fields.shape, BF16)...]
    dot_general x10 -> x0, matrix products: 67.9 us -> none  [the longest x1 27.7 us: spectral_block(): jnp.einsum('icq,ijq->icj', spectral * damping, basis, precision=lax.Preci...]
    unnamed x7 -> x1, local copies, waits for them, and re-layouts: 68.5 us -> 2.41 us
    all_to_all x3 -> x0, waiting for transfers between devices: 33.5 us -> none  [the longest x1 14.5 us: body(): lax.all_to_all(sending, ('lat', 'lev'), split_axis=0, concat_axis=0, tile...]
    all_to_all x8 -> x0, local copies, waits for them, and re-layouts: 30.1 us -> none  [the longest x3 19.3 us: body(): lax.all_to_all(grid_rows, 'lev', split_axis=2, concat_axis=1, tiled=True)]
  transfers between devices with their start and end apart: 3 -> 0, of which waited for: 3 -> 0; matrix products, arithmetic and copies ran while one was open for 2% -> 0% of each run, Pallas kernels for 0% -> 0%
where the time goes in v1:
time: 75.8 us; the launch traced here: 75.6 us
  Pallas kernels  73.2 us (97%)
  local copies, waits for them, and re-layouts  2.41 us (3%)
    pallas_call x1, Pallas kernels, body(): pl.pallas_call(kernel, out_shape=jax.ShapeDtypeStruct(fields.shape, BF16)...  73.2 us
    unnamed x1, local copies, waits for them, and re-layouts  2.41 us

profile of v1, /device:TPU:1, one launch (start us, length us, event | category | flops | bytes accessed | tf_op | source)
XLA Modules:
  0.0 75.6 jit_solution(17396413748965252027)
XLA Ops:
  0.0 73.2 %shard_map.73 = bf16[4,72,2048]{2,1,0:T(8,128)(2,1)} custom-call(s32[64]{0:T(128)} %lat_s.1, s32[64]{0:T(128)} %cnt_s.1, s32[2048]{0:T(1024)} %wave_s.1, f32[64]{0:T(128)} %wgt_s.1, f32[3]{0:T(128)} %dif_s.1, s32[1,2048]{1,0:T(1,128)} %bitcast.1, bf16[4,72,2048]{2,1,0:T(8,128)(2,1)} %fields.1, f32[16,64,2048]{2,1,0:T(8,128)} %leg_hbm.1), custom_call_target="tpu_custom_call" | custom-call | flops 20000000000 | bytes 12000000 | tf_op jit(solution)/shard_map/pallas_call | solution.py:355
  73.2 2.4 %copy.9 = bf16[4,72,2048]{2,1,0:T(8,128)(2,1)} copy(bf16[4,72,2048]{2,1,0:T(8,128)(2,1)} %shard_map.73) | data formatting | bytes 2359296

commit v2 on v1

v2 whole, which is shorter than its diff:
```python
import math

import jax
import jax.numpy as jnp
from jax import lax
from jax.experimental import pallas as pl
from jax.experimental.pallas import tpu as pltpu
from jax.sharding import PartitionSpec as P

F32, BF16 = jnp.float32, jnp.bfloat16
MESH = pl.DeviceIdType.MESH

M = 2048
N_LAT, N_LEV = 16, 8
DEV = N_LAT * N_LEV
NLAT = 64
LEV = 24
FL = 72
HALF = FL // 2
ROWS = NLAT // N_LAT
PTS = 2048
K0 = 256
KK = PTS // K0
PAIRS = KK // 2
EACH = M // DEV
WT = 256
LANES = 128
SIZES = (20, 16)
STARTS = (0, 20)
CHUNKS = range(len(SIZES))
SLOT = 64


def padded(rows):
    return -(-rows // 16) * 16


def nt_dot(a, b):
    return lax.dot_general(a, b, (((1,), (1,)), ((), ())), preferred_element_type=F32)


def sincos(wave, factor, count):
    product = wave * factor
    countf = count.astype(F32)
    turns = jnp.floor(product.astype(F32) * (1.0 / countf) + 0.5).astype(jnp.int32)
    rest = product - turns * count
    rest = jnp.where(2 * rest > count, rest - count, rest)
    rest = jnp.where(2 * rest < -count, rest + count, rest)
    z = rest.astype(F32) * (math.pi / countf)
    y = z * z
    s = jnp.full_like(y, 1.0 / math.factorial(13))
    for k in (11, 9, 7, 5, 3, 1):
        s = s * y + (-1.0) ** (k // 2) / math.factorial(k)
    s = s * z
    c = jnp.full_like(y, 1.0 / math.factorial(14) * -1.0)
    for k in (12, 10, 8, 6, 4, 2, 0):
        c = c * y + (-1.0) ** (k // 2) / math.factorial(k)
    return 1.0 - 2.0 * s * s, 2.0 * s * c


def kernel(
    lat_s, cnt_s, wave_s, wgt_s, dif_s, wave_v, fields, leg_hbm, out,
    leg, tmp, stages, xs, xr, basis, twc, tws, ebc, ebs, eac, eas, one,
    accr, acci, ft, fs, f1, mid, m1, f2, x32, y32, g1, g2, gs, g3,
    pm, cn, wt, bs, gst, ur, ui, ys, yr, o32,
    leg_sem, xs_sem, xr_sem, ys_sem, yr_sem, tile_sem,
):
    lat, lev = lax.axis_index("lat"), lax.axis_index("lev")
    z = lev // 2

    barrier = pltpu.get_barrier_semaphore()

    def greet_lev(d, carry):
        pl.semaphore_signal(
            barrier, inc=1, device_id=(lat, lax.rem(lev + d, N_LEV)), device_id_type=MESH
        )
        return carry

    def greet_lat(d, carry):
        pl.semaphore_signal(
            barrier, inc=1, device_id=(lax.rem(lat + d, N_LAT), lev), device_id_type=MESH
        )
        return carry

    lax.fori_loop(1, N_LEV, greet_lev, 0)
    lax.fori_loop(1, N_LAT, greet_lat, 0)
    leg_copy = pltpu.make_async_copy(leg_hbm, leg, leg_sem)
    leg_copy.start()

    lane = lax.broadcasted_iota(jnp.int32, (FL, K0), 1)

    def stage_row(t, carry):
        count = cnt_s[lat_s[ROWS * lat + t]]
        for kk in range(KK):
            x = fields[t, :, kk * K0 : (kk + 1) * K0].astype(F32)
            tmp[kk % 2] = jnp.where(lane + (lev * PTS + kk * K0) < count, x, 0.0)
            for n in CHUNKS:
                for h in range(2):
                    first = h * HALF + STARTS[n]
                    stages[n][h, kk * SIZES[n] : (kk + 1) * SIZES[n], :] = tmp[
                        kk % 2, first : first + SIZES[n], :
                    ]
        for n in CHUNKS:
            for h in range(2):
                xs[n][2 * t + h] = stages[n][h].astype(BF16)
        return carry

    lax.fori_loop(0, ROWS, stage_row, 0)

    pl.semaphore_wait(barrier, N_LEV - 1 + N_LAT - 1)

    def x_copy(n, target, source):
        return pltpu.make_async_remote_copy(
            src_ref=xs[n].at[target],
            dst_ref=xr[n].at[source],
            send_sem=xs_sem.at[n, target],
            recv_sem=xr_sem.at[n, source],
            device_id=(lat, target),
            device_id_type=MESH,
        )

    other = lev + 1 - 2 * lax.rem(lev, 2)

    def partner(step):
        chip_step = step // 2
        far = jnp.where(chip_step == 0, 1, jnp.where(chip_step == 1, 3, 2))
        return 2 * lax.rem(z + far, 4) + lax.rem(lev + lax.rem(step, 2), 2)

    for n in CHUNKS:
        x_copy(n, other, lev).start()

        def send_x(step, carry, n=n):
            x_copy(n, partner(step), lev).start()
            return carry

        lax.fori_loop(0, 6, send_x, 0)

    count = cnt_s[lat_s[ROWS * lat + z]]
    waves16 = jnp.broadcast_to(wave_v[...], (16, M))
    row16 = lax.broadcasted_iota(jnp.int32, (16, M), 0)
    ebc[...], ebs[...] = sincos(waves16, row16, count)
    eac[...], eas[...] = sincos(waves16, row16 * 16, count)
    twc[0:16], tws[0:16] = sincos(waves16, row16 * (2 * K0), count)
    twc[16:32], tws[16:32] = sincos(waves16, row16 * (2 * K0) + 32 * K0, count)
    waves8 = jnp.broadcast_to(wave_v[...], (8, M))
    one[0], one[1] = sincos(waves8, jnp.full((8, M), K0, jnp.int32), count)

    def basis_rows(a, carry):
        ca, sa = eac[pl.ds(a, 1), :], eas[pl.ds(a, 1), :]
        cb, sb = ebc[...], ebs[...]
        rows = pl.ds(pl.multiple_of(a * 16, 16), 16)
        basis[rows, 0:M] = (ca * cb - sa * sb).astype(BF16)
        basis[rows, M : 2 * M] = (-(sa * cb + ca * sb)).astype(BF16)
        return carry

    lax.fori_loop(0, 16, basis_rows, 0)

    lane64 = lax.broadcasted_iota(jnp.int32, (1, NLAT), 1)

    def slot_row(t, carry):
        j = lat_s[t]
        row = pl.ds(t, 1)
        pm[row, :] = jnp.where(lane64 == j, 1.0, 0.0)
        cn[row, :] = jnp.full((1, NLAT), cnt_s[j], jnp.int32).astype(F32)
        wt[row, :] = jnp.full((1, NLAT), wgt_s[j], F32)
        return carry

    lax.fori_loop(0, NLAT, slot_row, 0)
    eye = lax.broadcasted_iota(jnp.int32, (NLAT, NLAT), 0) == lax.broadcasted_iota(
        jnp.int32, (NLAT, NLAT), 1
    )
    count_col = cn[...]
    count_row = jnp.sum(jnp.where(eye, count_col, 0.0), axis=0, keepdims=True)
    share_row = jnp.sum(jnp.where(eye, wt[...], 0.0), axis=0, keepdims=True) / count_row
    perm = pm[...].astype(BF16)
    degree = lax.broadcasted_iota(jnp.int32, (1, M), 1)
    leg_copy.wait()

    def operator(i, carry):
        m = wave_s[(lat * N_LEV + lev) * EACH + i]
        deg = (degree + m).astype(F32)
        scaled = deg * (deg + 1.0) * (1.0 / float(M * (M - 1)))
        scaled = scaled * scaled
        own = jnp.dot(perm, leg[i].astype(BF16), preferred_element_type=F32)
        for f in range(3):
            bs[f * NLAT : (f + 1) * NLAT, :] = (own * (1.0 / (1.0 + dif_s[f] * scaled))).astype(BF16)
        g = nt_dot(bs[...], own.astype(BF16))
        twice_m = (2 * jnp.full((1, NLAT), m, jnp.int32)).astype(F32)
        from_row = jnp.where(twice_m < count_row, share_row, 0.0)
        to_col = jnp.where(twice_m < count_col, jnp.where(twice_m == 0.0, 1.0, 2.0), 0.0)
        scale = to_col * from_row
        for f in range(3):
            gst[i, f * NLAT : (f + 1) * NLAT, :] = (g[f * NLAT : (f + 1) * NLAT, :] * scale).astype(BF16)
        return carry

    lax.fori_loop(0, EACH, operator, 0)

    x32[...] = jnp.zeros_like(x32)
    ft[...] = jnp.zeros_like(ft)
    c1, s1 = one[0, 0:1, :], one[1, 0:1, :]

    def xy_copy(n, k, source, target_ref, d):
        target = lax.rem(lat + d, N_LAT)
        return pltpu.make_async_remote_copy(
            src_ref=source.at[target],
            dst_ref=target_ref.at[lat],
            send_sem=tile_sem.at[n, k, 0],
            recv_sem=tile_sem.at[n, k, 1],
            device_id=(target, lev),
            device_id_type=MESH,
        )

    def xy_send(n, k, source, target_ref):
        def step(d, carry):
            xy_copy(n, k, source, target_ref, d).start()
            return carry

        lax.fori_loop(1, N_LAT, step, 0)
        target_ref[lat] = source[lat]

    def xy_all(n, k, source, target_ref):
        return pltpu.make_async_remote_copy(
            src_ref=source.at[pl.ds(0, N_LAT - 1)],
            dst_ref=target_ref.at[pl.ds(0, N_LAT - 1)],
            send_sem=tile_sem.at[n, k, 0],
            recv_sem=tile_sem.at[n, k, 1],
            device_id=(lax.rem(lat + 1, N_LAT), lev),
            device_id_type=MESH,
        )

    def slab(index):
        return pl.ds(pl.multiple_of(index * EACH, EACH), EACH)

    def z_send(n, k, source, target_ref):
        def step(d, carry):
            target = lax.rem(lev + d, N_LEV)
            pltpu.make_async_remote_copy(
                src_ref=source.at[slab(target), :],
                dst_ref=target_ref.at[slab(lev), :],
                send_sem=tile_sem.at[n, k, 0],
                recv_sem=tile_sem.at[n, k, 1],
                device_id=(lat, target),
                device_id_type=MESH,
            ).start()
            return carry

        lax.fori_loop(1, N_LEV, step, 0)
        target_ref[slab(lev), :] = source[slab(lev), :]

    def z_all(n, k, source, target_ref):
        whole = pl.ds(0, (N_LEV - 1) * EACH)
        return pltpu.make_async_remote_copy(
            src_ref=source.at[whole, :],
            dst_ref=target_ref.at[whole, :],
            send_sem=tile_sem.at[n, k, 0],
            recv_sem=tile_sem.at[n, k, 1],
            device_id=(lat, lax.rem(lev + 1, N_LEV)),
            device_id_type=MESH,
        )

    def chip_at(step):
        far = jnp.where(step == 0, 0, jnp.where(step == 1, 3, jnp.where(step == 2, 1, 2)))
        return lax.rem(z + far, 4)

    def forward_start(n):
        accr[n][...] = jnp.zeros_like(accr[n])
        acci[n][...] = jnp.zeros_like(acci[n])
        xr[n][lev] = xs[n][lev]

    def forward(n, first, last):
        columns = 2 * SIZES[n]

        def step(index, carry):
            chip = chip_at(index)
            for q in range(2):
                p = 2 * chip + q

                @pl.when(p != lev)
                def _(p=p):
                    x_copy(n, p, p).wait_recv()

            points = xr[n][pl.ds(2 * chip, 2)].reshape(2 * KK * SIZES[n], K0)
            for w in range(M // WT):
                cols = slice(w * WT, (w + 1) * WT)
                pr = jnp.dot(points, basis[:, cols], preferred_element_type=F32)
                pi = jnp.dot(points, basis[:, M + w * WT : M + (w + 1) * WT], preferred_element_type=F32)
                ar, ai = accr[n][:, cols], acci[n][:, cols]
                for k in range(2 * PAIRS):
                    c = twc[pl.ds(chip * (2 * PAIRS) + k, 1), cols]
                    s = tws[pl.ds(chip * (2 * PAIRS) + k, 1), cols]
                    br, bi = pr[k * columns : (k + 1) * columns], pi[k * columns : (k + 1) * columns]
                    ar = ar + (br * c + bi * s)
                    ai = ai + (bi * c - br * s)
                accr[n][:, cols] = ar
                acci[n][:, cols] = ai
            return carry

        lax.fori_loop(first, last, step, 0)

    def forward_end(n):
        size, columns = SIZES[n], 2 * SIZES[n]
        odd_r, odd_i = accr[n][size:columns, :], acci[n][size:columns, :]
        ft[0:size, :] = accr[n][0:size, :] + (odd_r * c1 + odd_i * s1)
        ft[size:columns, :] = acci[n][0:size, :] + (odd_i * c1 - odd_r * s1)
        for w in range(N_LAT):
            fs[n][w] = ft[0 : padded(columns), w * LANES : (w + 1) * LANES].astype(BF16)
        xy_send(n, 0, fs[n], f1[n])

    def middle(n):
        columns = 2 * SIZES[n]
        xy_all(n, 0, fs[n], f1[n]).wait_recv()
        for r in range(N_LAT):
            mid[r * columns : (r + 1) * columns, :] = f1[n][r].astype(F32)[0:columns, :]
        for j in range(N_LAT * columns // LANES):
            cols = slice(j * LANES, (j + 1) * LANES)
            m1[n][:, cols] = mid[cols, :].T.astype(BF16)
        z_send(n, 1, m1[n], f2[n])

    def apply(n):
        size, columns = SIZES[n], 2 * SIZES[n]
        z_all(n, 1, m1[n], f2[n]).wait_recv()
        for source in range(N_LEV):
            v = f2[n][source * EACH : (source + 1) * EACH, :].astype(F32)
            lanes = slice((source % 2) * SLOT, (source % 2) * SLOT + columns)
            for r in range(N_LAT):
                t = r * ROWS + source // 2
                x32[t * EACH : (t + 1) * EACH, lanes] = v[:, r * columns : (r + 1) * columns]
        column = lax.broadcasted_iota(jnp.int32, (NLAT, LANES), 1)
        level = STARTS[n] + jnp.where(column >= SLOT, column - SLOT + HALF, column)
        inside = jnp.where(column >= SLOT, column - SLOT, column)
        level = jnp.where(inside >= size, level - size, level)
        for i in range(EACH):
            x = x32[pl.ds(i, NLAT, stride=EACH), :].astype(BF16)
            y = jnp.dot(gst[i], x, preferred_element_type=F32)
            y32[pl.ds(i, NLAT, stride=EACH), :] = jnp.where(
                level < LEV, y[0:NLAT], jnp.where(level < 2 * LEV, y[NLAT : 2 * NLAT], y[2 * NLAT :])
            )
        for target in range(N_LEV):
            lanes = slice((target % 2) * SLOT, (target % 2) * SLOT + columns)
            pieces = []
            for r in range(N_LAT):
                t = r * ROWS + target // 2
                pieces.append(y32[t * EACH : (t + 1) * EACH, lanes])
            g1[n][target * EACH : (target + 1) * EACH, :] = jnp.concatenate(pieces, axis=1).astype(BF16)
        z_send(n, 2, g1[n], g2[n])

    def middle_back(n):
        columns = 2 * SIZES[n]
        z_all(n, 2, g1[n], g2[n]).wait_recv()
        for j in range(N_LAT * columns // LANES):
            cols = slice(j * LANES, (j + 1) * LANES)
            mid[cols, :] = g2[n][:, cols].astype(F32).T
        for r in range(N_LAT):
            block = mid[r * columns : (r + 1) * columns, :]
            if padded(columns) > columns:
                block = jnp.concatenate([block, jnp.zeros((padded(columns) - columns, LANES), F32)], axis=0)
            gs[n][r] = block.astype(BF16)
        xy_send(n, 3, gs[n], g3[n])

    def inverse_start(n):
        size, columns = SIZES[n], 2 * SIZES[n]
        xy_all(n, 3, gs[n], g3[n]).wait_recv()
        for w in range(N_LAT):
            ft[0:columns, w * LANES : (w + 1) * LANES] = g3[n][w].astype(F32)[0:columns, :]
        re, im = ft[0:size, :], ft[size:columns, :]
        ur[n][0:size, :] = re
        ui[n][0:size, :] = im
        ur[n][size:columns, :] = re * c1 - im * s1
        ui[n][size:columns, :] = re * s1 + im * c1

    def y_copy(n, target, source):
        return pltpu.make_async_remote_copy(
            src_ref=ys[n].at[target],
            dst_ref=yr[n].at[source],
            send_sem=ys_sem.at[n, target],
            recv_sem=yr_sem.at[n, source],
            device_id=(lat, target),
            device_id_type=MESH,
        )

    def inverse(n, first, last):
        rows = 2 * KK * SIZES[n]
        row = lax.broadcasted_iota(jnp.int32, (rows, K0), 0)
        point = lax.broadcasted_iota(jnp.int32, (rows, K0), 1)
        for kk in range(1, 2 * KK):
            point = point + jnp.where(row >= kk * SIZES[n], K0, 0)

        def step(index, carry):
            chip = chip_at(3 - index)
            total = jnp.zeros((rows, K0), F32)
            for w in range(M // WT):
                cols = slice(w * WT, (w + 1) * WT)
                vr, vi = ur[n][:, cols], ui[n][:, cols]
                tr, ti = [], []
                for k in range(2 * PAIRS):
                    c = twc[pl.ds(chip * (2 * PAIRS) + k, 1), cols]
                    s = tws[pl.ds(chip * (2 * PAIRS) + k, 1), cols]
                    tr.append(vr * c - vi * s)
                    ti.append(vr * s + vi * c)
                total = total + nt_dot(jnp.concatenate(tr, axis=0).astype(BF16), basis[:, cols])
                total = total + nt_dot(
                    jnp.concatenate(ti, axis=0).astype(BF16), basis[:, M + w * WT : M + (w + 1) * WT]
                )
            total = jnp.where(point + chip * (2 * PTS) < count, total, 0.0).astype(BF16)
            for q in range(2):
                p = 2 * chip + q
                ys[n][p] = total[q * (rows // 2) : (q + 1) * (rows // 2)]

                @pl.when(p != lev)
                def _(p=p):
                    y_copy(n, p, lev).start()

            return carry

        lax.fori_loop(first, last, step, 0)

    forward_start(0)
    forward(0, 0, 4)
    forward_end(0)
    forward_start(1)
    forward(1, 0, 1)
    middle(0)
    forward(1, 1, 4)
    forward_end(1)
    apply(0)
    middle(1)
    middle_back(0)
    apply(1)
    inverse_start(0)
    inverse(0, 0, 2)
    middle_back(1)
    inverse(0, 2, 4)
    inverse_start(1)
    inverse(1, 0, 4)

    for n in CHUNKS:
        yr[n][lev] = ys[n][lev]

        def waited(d, carry, n=n):
            y_copy(n, lev, lax.rem(lev + d, N_LEV)).wait_recv()
            return carry

        lax.fori_loop(1, N_LEV, waited, 0)

    def finish_row(t, carry):
        for n in CHUNKS:
            for h in range(2):
                stages[n][h] = yr[n][2 * t + h].astype(F32)
                first = h * HALF + STARTS[n]
                for kk in range(KK):
                    o32[first : first + SIZES[n], kk * K0 : (kk + 1) * K0] = stages[n][
                        h, kk * SIZES[n] : (kk + 1) * SIZES[n], :
                    ]
        out[t] = o32[...].astype(BF16)
        return carry

    lax.fori_loop(0, ROWS, finish_row, 0)

    for n in CHUNKS:

        def sent(d, carry, n=n):
            target = lax.rem(lev + d, N_LEV)
            x_copy(n, target, lev).wait_send()
            y_copy(n, target, lev).wait_send()
            return carry

        lax.fori_loop(1, N_LEV, sent, 0)
        xy_all(n, 0, fs[n], f1[n]).wait_send()
        z_all(n, 1, m1[n], f2[n]).wait_send()
        z_all(n, 2, g1[n], g2[n]).wait_send()
        xy_all(n, 3, gs[n], g3[n]).wait_send()


def body(fields, lat_order, counts, wave_order, weights, diffusion, legendre):
    smem, vmem = pl.BlockSpec(memory_space=pltpu.SMEM), pl.BlockSpec(memory_space=pltpu.VMEM)
    dma = pltpu.SemaphoreType.DMA

    def each(shape, dtype):
        return tuple(pltpu.VMEM(shape(size), dtype) for size in SIZES)

    block = each(lambda size: (N_LEV, KK * size, K0), BF16)
    acc = each(lambda size: (2 * size, M), F32)
    tiles = each(lambda size: (N_LAT, padded(2 * size), LANES), BF16)
    slabs = each(lambda size: (LANES, N_LAT * 2 * size), BF16)
    table = pltpu.VMEM((16, M), F32)
    square = pltpu.VMEM((NLAT, NLAT), F32)
    owned = pltpu.VMEM((NLAT * EACH, LANES), F32)
    return pl.pallas_call(
        kernel,
        out_shape=jax.ShapeDtypeStruct(fields.shape, BF16),
        in_specs=[smem] * 5 + [vmem, vmem, pl.BlockSpec(memory_space=pl.ANY)],
        out_specs=vmem,
        scratch_shapes=[
            pltpu.VMEM((EACH, NLAT, M), F32),
            pltpu.VMEM((2, FL, K0), F32),
            each(lambda size: (2, KK * size, K0), F32),
            block, block,
            pltpu.VMEM((K0, 2 * M), BF16),
            pltpu.VMEM((32, M), F32), pltpu.VMEM((32, M), F32),
            table, table, table, table,
            pltpu.VMEM((2, 8, M), F32),
            acc, acc,
            pltpu.VMEM((padded(2 * max(SIZES)), M), F32),
            tiles, tiles,
            pltpu.VMEM((N_LAT * 2 * max(SIZES), LANES), F32),
            slabs, slabs,
            owned, owned,
            slabs, slabs,
            tiles, tiles,
            square, square, square,
            pltpu.VMEM((3 * NLAT, M), BF16),
            pltpu.VMEM((EACH, 3 * NLAT, NLAT), BF16),
            acc, acc,
            block, block,
            pltpu.VMEM((FL, M), F32),
            dma,
            dma((2, N_LEV)), dma((2, N_LEV)), dma((2, N_LEV)), dma((2, N_LEV)),
            dma((2, 4, 2)),
        ],
        compiler_params=pltpu.CompilerParams(
            collective_id=0, has_side_effects=True, vmem_limit_bytes=56 * 1024 * 1024
        ),
        cost_estimate=pl.CostEstimate(
            flops=20_000_000_000, bytes_accessed=12_000_000, transcendentals=0
        ),
    )(lat_order, counts, wave_order, weights, diffusion, wave_order.reshape(1, M), fields, legendre)


def solution(mesh):
    placed = (P("lat", None, "lev"), P(), P(), P(), P(), P(), P(("lat", "lev"), None, None))
    return jax.shard_map(
        body, mesh=mesh, in_specs=placed, out_specs=P("lat", None, "lev"), check_vma=False
    )
```

time: 75.8 us -> 66.9 us (0.88)
  Pallas kernels: 73.2 us -> 64.3 us
    pallas_call x1, Pallas kernels: 73.2 us -> 64.3 us  [body(): pl.pallas_call(kernel, out_shape=jax.ShapeDtypeStruct(fields.shape, BF16)...]
where the time goes in v2:
time: 66.9 us; the launch traced here: 66.7 us
  Pallas kernels  64.3 us (96%)
  local copies, waits for them, and re-layouts  2.41 us (4%)
    pallas_call x1, Pallas kernels, body(): pl.pallas_call(kernel, out_shape=jax.ShapeDtypeStruct(fields.shape, BF16)...  64.3 us
    unnamed x1, local copies, waits for them, and re-layouts  2.41 us

profile of v2, /device:TPU:1, one launch (start us, length us, event | category | flops | bytes accessed | tf_op | source)
XLA Modules:
  0.0 66.7 jit_solution(813789587579862105)
XLA Ops:
  0.0 64.3 %shard_map.73 = bf16[4,72,2048]{2,1,0:T(8,128)(2,1)} custom-call(s32[64]{0:T(128)} %lat_s.1, s32[64]{0:T(128)} %cnt_s.1, s32[2048]{0:T(1024)} %wave_s.1, f32[64]{0:T(128)} %wgt_s.1, f32[3]{0:T(128)} %dif_s.1, s32[1,2048]{1,0:T(1,128)} %bitcast.1, bf16[4,72,2048]{2,1,0:T(8,128)(2,1)} %fields.1, f32[16,64,2048]{2,1,0:T(8,128)} %leg_hbm.1), custom_call_target="tpu_custom_call" | custom-call | flops 20000000000 | bytes 12000000 | tf_op jit(solution)/shard_map/pallas_call | solution.py:488
  64.3 2.4 %copy.9 = bf16[4,72,2048]{2,1,0:T(8,128)(2,1)} copy(bf16[4,72,2048]{2,1,0:T(8,128)(2,1)} %shard_map.73) | data formatting | bytes 2359296

commit v3 on v2

--- a/solution.py
+++ b/solution.py
@@ -126,14 +126,16 @@
         far = jnp.where(chip_step == 0, 1, jnp.where(chip_step == 1, 3, 2))
         return 2 * lax.rem(z + far, 4) + lax.rem(lev + lax.rem(step, 2), 2)
 
-    for n in CHUNKS:
+    def points_send(n):
         x_copy(n, other, lev).start()
 
-        def send_x(step, carry, n=n):
+        def send_x(step, carry):
             x_copy(n, partner(step), lev).start()
             return carry
 
         lax.fori_loop(0, 6, send_x, 0)
+
+    points_send(0)
 
     count = cnt_s[lat_s[ROWS * lat + z]]
     waves16 = jnp.broadcast_to(wave_v[...], (16, M))
@@ -193,7 +195,8 @@
             gst[i, f * NLAT : (f + 1) * NLAT, :] = (g[f * NLAT : (f + 1) * NLAT, :] * scale).astype(BF16)
         return carry
 
-    lax.fori_loop(0, EACH, operator, 0)
+    def operators(first, last):
+        lax.fori_loop(first, last, operator, 0)
 
     x32[...] = jnp.zeros_like(x32)
     ft[...] = jnp.zeros_like(ft)
@@ -414,9 +417,12 @@
 
         lax.fori_loop(first, last, step, 0)
 
+    operators(0, 8)
+    points_send(1)
     forward_start(0)
     forward(0, 0, 4)
     forward_end(0)
+    operators(8, 16)
     forward_start(1)
     forward(1, 0, 1)
     middle(0)

time: 66.9 us -> 62.6 us (0.936)
  Pallas kernels: 64.3 us -> 60 us
    pallas_call x1, Pallas kernels: 64.3 us -> 60 us  [body(): pl.pallas_call(kernel, out_shape=jax.ShapeDtypeStruct(fields.shape, BF16)...]
where the time goes in v3:
time: 62.6 us; the launch traced here: 62.4 us
  Pallas kernels  60 us (96%)
  local copies, waits for them, and re-layouts  2.41 us (4%)
    pallas_call x1, Pallas kernels, body(): pl.pallas_call(kernel, out_shape=jax.ShapeDtypeStruct(fields.shape, BF16)...  60 us
    unnamed x1, local copies, waits for them, and re-layouts  2.41 us

profile of v3, /device:TPU:1, one launch (start us, length us, event | category | flops | bytes accessed | tf_op | source)
XLA Modules:
  0.0 62.4 jit_solution(12181895274018420855)
XLA Ops:
  0.0 60.0 %shard_map.73 = bf16[4,72,2048]{2,1,0:T(8,128)(2,1)} custom-call(s32[64]{0:T(128)} %lat_s.1, s32[64]{0:T(128)} %cnt_s.1, s32[2048]{0:T(1024)} %wave_s.1, f32[64]{0:T(128)} %wgt_s.1, f32[3]{0:T(128)} %dif_s.1, s32[1,2048]{1,0:T(1,128)} %bitcast.1, bf16[4,72,2048]{2,1,0:T(8,128)(2,1)} %fields.1, f32[16,64,2048]{2,1,0:T(8,128)} %leg_hbm.1), custom_call_target="tpu_custom_call" | custom-call | flops 20000000000 | bytes 12000000 | tf_op jit(solution)/shard_map/pallas_call | solution.py:494
  60.0 2.4 %copy.9 = bf16[4,72,2048]{2,1,0:T(8,128)(2,1)} copy(bf16[4,72,2048]{2,1,0:T(8,128)(2,1)} %shard_map.73) | data formatting | bytes 2359296

commit v4 on v3

--- a/solution.py
+++ b/solution.py
@@ -423,10 +423,9 @@
     forward(0, 0, 4)
     forward_end(0)
     operators(8, 16)
+    middle(0)
     forward_start(1)
-    forward(1, 0, 1)
-    middle(0)
-    forward(1, 1, 4)
+    forward(1, 0, 4)
     forward_end(1)
     apply(0)
     middle(1)

time: 62.6 us -> 62 us (level)
  no operation moved by 1% of the time
where the time goes in v4:
time: 62 us; the launch traced here: 61.9 us
  Pallas kernels  59.4 us (96%)
  local copies, waits for them, and re-layouts  2.41 us (4%)
    pallas_call x1, Pallas kernels, body(): pl.pallas_call(kernel, out_shape=jax.ShapeDtypeStruct(fields.shape, BF16)...  59.4 us
    unnamed x1, local copies, waits for them, and re-layouts  2.41 us

profile of v4, /device:TPU:1, one launch (start us, length us, event | category | flops | bytes accessed | tf_op | source)
XLA Modules:
  0.0 61.9 jit_solution(9767577087245558940)
XLA Ops:
  0.0 59.4 %shard_map.73 = bf16[4,72,2048]{2,1,0:T(8,128)(2,1)} custom-call(s32[64]{0:T(128)} %lat_s.1, s32[64]{0:T(128)} %cnt_s.1, s32[2048]{0:T(1024)} %wave_s.1, f32[64]{0:T(128)} %wgt_s.1, f32[3]{0:T(128)} %dif_s.1, s32[1,2048]{1,0:T(1,128)} %bitcast.1, bf16[4,72,2048]{2,1,0:T(8,128)(2,1)} %fields.1, f32[16,64,2048]{2,1,0:T(8,128)} %leg_hbm.1), custom_call_target="tpu_custom_call" | custom-call | flops 20000000000 | bytes 12000000 | tf_op jit(solution)/shard_map/pallas_call | solution.py:493
  59.5 2.4 %copy.9 = bf16[4,72,2048]{2,1,0:T(8,128)(2,1)} copy(bf16[4,72,2048]{2,1,0:T(8,128)(2,1)} %shard_map.73) | data formatting | bytes 2359296

commit v5 on v4

--- a/solution.py
+++ b/solution.py
@@ -417,12 +417,12 @@
 
         lax.fori_loop(first, last, step, 0)
 
-    operators(0, 8)
+    operators(0, 10)
     points_send(1)
     forward_start(0)
     forward(0, 0, 4)
     forward_end(0)
-    operators(8, 16)
+    operators(10, 16)
     middle(0)
     forward_start(1)
     forward(1, 0, 4)

time: 62 us -> 63.4 us (1.023)
  Pallas kernels: 59.4 us -> 60.8 us
    pallas_call x1, Pallas kernels: 59.4 us -> 60.8 us  [body(): pl.pallas_call(kernel, out_shape=jax.ShapeDtypeStruct(fields.shape, BF16)...]
where the time goes in v5:
time: 63.4 us; the launch traced here: 63.2 us
  Pallas kernels  60.8 us (96%)
  local copies, waits for them, and re-layouts  2.41 us (4%)
    pallas_call x1, Pallas kernels, body(): pl.pallas_call(kernel, out_shape=jax.ShapeDtypeStruct(fields.shape, BF16)...  60.8 us
    unnamed x1, local copies, waits for them, and re-layouts  2.41 us

profile of v5, /device:TPU:1, one launch (start us, length us, event | category | flops | bytes accessed | tf_op | source)
XLA Modules:
  0.0 63.2 jit_solution(17048747417363900351)
XLA Ops:
  0.0 60.8 %shard_map.73 = bf16[4,72,2048]{2,1,0:T(8,128)(2,1)} custom-call(s32[64]{0:T(128)} %lat_s.1, s32[64]{0:T(128)} %cnt_s.1, s32[2048]{0:T(1024)} %wave_s.1, f32[64]{0:T(128)} %wgt_s.1, f32[3]{0:T(128)} %dif_s.1, s32[1,2048]{1,0:T(1,128)} %bitcast.1, bf16[4,72,2048]{2,1,0:T(8,128)(2,1)} %fields.1, f32[16,64,2048]{2,1,0:T(8,128)} %leg_hbm.1), custom_call_target="tpu_custom_call" | custom-call | flops 20000000000 | bytes 12000000 | tf_op jit(solution)/shard_map/pallas_call | solution.py:493
  60.8 2.4 %copy.9 = bf16[4,72,2048]{2,1,0:T(8,128)(2,1)} copy(bf16[4,72,2048]{2,1,0:T(8,128)(2,1)} %shard_map.73) | data formatting | bytes 2359296
